TPU v7x, 256 devices: a whole 4x4x8 slice. The times are simulated.
256 devices in a mesh: rows: 64 (over z, x, core), cols: 4 (over y).
Axes of the slice: x: 4, y: 4, z: 8, core: 2. Of those that a mesh axis runs over, the one named last changes fastest.
Arguments:
- tiles: bfloat16 [64, 4, 32, 128, 128], P('rows', 'cols'), may hold values from -3 to 3
- tile_rows: int32 [64, 4, 32], P('rows', 'cols'), may hold values from 0 to 15
- tile_cols: int32 [64, 4, 32], P('rows', 'cols'), may hold values from 0 to 15
- tile_counts: int32 [64, 4], P('rows', 'cols'), may hold values from 16 to 32, as said below
- sketch: bfloat16 [4, 2048, 256], P('cols', 'rows'), may hold values from -6 to 6
Outputs:
- basis: float32 [131072, 256], P(('rows', 'cols'))
- factor: float32 [256, 256], replicated
Inputs may be any that keep to these rules, and one draw needn't show every extreme that they name: The live slots of a slab and column group are its first tile_counts slots; some slab and group has all 32 slots live.
All inputs are finite; a program needn't handle non-finite values.
Results may differ from a plain program's by a relative error of at most 0.004.
Values may be sent and summed in bfloat16 or wider, within the bound.
A program may use at most 64 MiB of HBM per device.

v0:
```python
import jax
import jax.numpy as jnp
from jax import lax
from jax.sharding import PartitionSpec as P

ROUNDS = 2
TR = 16
CGT = 16


def tile_product(blocks, rows_idx, cols_idx, live, xgroup):
    width = blocks.shape[1]
    rank = xgroup.shape[-1]
    picked = xgroup.reshape(-1, width, rank)[cols_idx]
    prods = jnp.einsum("tij,tjk->tik", blocks, picked, preferred_element_type=jnp.float32)
    onehot = (
        (rows_idx[None, :] == jnp.arange(TR, dtype=jnp.int32)[:, None]) & live[None, :]
    ).astype(jnp.float32)
    return jnp.einsum("rt,tik->rik", onehot, prods, precision=lax.Precision.HIGHEST).reshape(
        -1, rank
    )


def tile_transposed(blocks, rows_idx, cols_idx, live, qslab):
    width = blocks.shape[1]
    rank = qslab.shape[-1]
    picked = qslab.reshape(-1, width, rank)[rows_idx]
    prods = jnp.einsum("tij,tik->tjk", blocks, picked, preferred_element_type=jnp.float32)
    onehot = (
        (cols_idx[None, :] == jnp.arange(CGT, dtype=jnp.int32)[:, None]) & live[None, :]
    ).astype(jnp.float32)
    return jnp.einsum("ct,tjk->cjk", onehot, prods, precision=lax.Precision.HIGHEST).reshape(
        -1, rank
    )


def lower_factor(gram):
    lower = jnp.linalg.cholesky(gram)
    inverse = jax.scipy.linalg.solve_triangular(
        lower, jnp.eye(gram.shape[0], dtype=jnp.float32), lower=True
    )
    return (lower, inverse)


def inner_gram(matrix):
    return jnp.dot(matrix.T, matrix, precision=lax.Precision.HIGHEST)


def shards(tiles, tile_rows, tile_cols, tile_counts, sketch):
    blocks = tiles[0, 0]
    rows_idx = tile_rows[0, 0]
    cols_idx = tile_cols[0, 0]
    live = jnp.arange(blocks.shape[0], dtype=jnp.int32) < tile_counts[0, 0]
    width = blocks.shape[1]
    slab_rows = TR * width
    group_cols = CGT * width
    total_rows = slab_rows * lax.axis_size("rows")
    total_cols = group_cols * lax.axis_size("cols")

    def row_side(xpiece, need_slab):
        xgroup = lax.all_gather(xpiece, "rows", axis=1, tiled=True)[0]
        partial_value = tile_product(blocks, rows_idx, cols_idx, live, xgroup)
        shares = lax.psum_scatter(partial_value, "cols", scatter_dimension=0, tiled=True)
        gram = lax.psum(inner_gram(shares), ("rows", "cols"))
        lower, inverse = lower_factor(gram / total_rows)
        mine = jnp.dot(shares, inverse.T, precision=lax.Precision.HIGHEST)
        slab_q = (
            lax.all_gather(mine.astype(jnp.bfloat16), "cols", axis=0, tiled=True)
            if need_slab
            else None
        )
        return (slab_q, mine, lower)

    slab_q, mine, lower = row_side(sketch, True)
    for step in range(ROUNDS):
        column_partial_value = tile_transposed(blocks, rows_idx, cols_idx, live, slab_q)
        column_shares = lax.psum_scatter(
            column_partial_value, "rows", scatter_dimension=0, tiled=True
        )
        column_gram = lax.psum(inner_gram(column_shares), ("rows", "cols"))
        column_lower, column_inverse = lower_factor(column_gram / total_cols)
        ortho = jnp.dot(column_shares, column_inverse.T, precision=lax.Precision.HIGHEST)
        xpiece = ortho.astype(jnp.bfloat16)[None]
        slab_q, mine, lower = row_side(xpiece, step + 1 < ROUNDS)
    return (mine, lower.T)


def solution(mesh):
    return jax.shard_map(
        shards,
        mesh=mesh,
        in_specs=(
            P("rows", "cols", None, None, None),
            P("rows", "cols", None),
            P("rows", "cols", None),
            P("rows", "cols"),
            P("cols", "rows", None),
        ),
        out_specs=(P(("rows", "cols"), None), P()),
        check_vma=False,
    )
```

profile of v0, /device:TPU:1, one launch (start us, length us, event | category | flops | bytes accessed | tf_op | source)
XLA Modules:
  0.0 2357.0 jit_solution(7003726758785728376)
XLA Ops:
  9.3 82.1 %all-gather.8.cloned.1.call-done = bf16[1,2048,256]{2,1,0:T(8,128)(2,1)} async-done(((bf16[1,32,256]{2,1,0:T(8,128)(2,1)}), bf16[1,2048,256]{2,1,0:T(8,128)(2,1)}) %all-gather.8.cloned.1.call-update) | async-done | bytes 1048592 | tf_op jit(solution)/shard_map/all_gather | solution.py:61
  96.0 5.5 copy.34
  101.5 3.8 fusion.8
  107.9 29.7 %reduce-scatter.6.cloned.1.call-done = f32[512,256]{1,0:T(8,128)} async-done(((f32[2048,256]{1,0:T(8,128)}), f32[512,256]{1,0:T(8,128)}) %reduce-scatter.6.cloned.1.call-update) | async-done | bytes 524304 | tf_op jit(solution)/shard_map/reduce_scatter | solution.py:63
  140.8 252.3 %all-reduce.7.cloned.1.call-done = f32[256,256]{0,1:T(8,128)} async-done(((f32[256,256]{0,1:T(8,128)}), f32[256,256]{0,1:T(8,128)}) %all-reduce.7.cloned.1.call-update) | async-done | bytes 262160 | tf_op jit(solution)/shard_map/psum | solution.py:64
  395.3 11.7 cholesky.256
  407.0 9.8 custom-call.19
  417.4 11.7 cholesky.273
  431.3 4.4 while.10
  435.7 19.7 custom-call.20
  457.7 25.8 %all-gather.10.cloned.1.call-done = bf16[2048,256]{1,0:T(8,128)(2,1)} async-done(((bf16[512,256]{1,0:T(8,128)(2,1)}), bf16[2048,256]{1,0:T(8,128)(2,1)}) %all-gather.10.cloned.1.call-update) | async-done | bytes 1048592 | tf_op jit(solution)/shard_map/all_gather | solution.py:68
  488.1 5.5 copy.36
  493.6 3.8 fusion.6
  500.0 136.9 %reduce-scatter.8.cloned.1.call-done = f32[32,256]{1,0:T(8,128)} async-done(((f32[2048,256]{1,0:T(8,128)}), f32[32,256]{1,0:T(8,128)}) %reduce-scatter.8.cloned.1.call-update) | async-done | bytes 32784 | tf_op jit(solution)/shard_map/reduce_scatter | solution.py:77
  639.4 255.7 %all-reduce.9.cloned.1.call-done = f32[256,256]{0,1:T(8,128)} async-done(((f32[256,256]{0,1:T(8,128)}), f32[256,256]{0,1:T(8,128)}) %all-reduce.9.cloned.1.call-update) | async-done | bytes 262160 | tf_op jit(solution)/shard_map/psum | solution.py:80
  897.2 11.7 cholesky.290
  909.0 9.8 custom-call.21
  919.2 11.7 cholesky.307
  933.8 4.3 while.11
  938.0 19.7 custom-call.22
  959.7 76.9 %all-gather.14.cloned.1.call-done = bf16[2048,256]{1,0:T(8,128)(2,1)} async-done(((bf16[32,256]{1,0:T(8,128)(2,1)}), bf16[2048,256]{1,0:T(8,128)(2,1)}) %all-gather.14.cloned.1.call-update) | async-done | bytes 1048592 | tf_op jit(solution)/shard_map/all_gather | solution.py:61
  1041.2 5.5 copy.38
  1046.7 3.8 fusion.4
  1053.1 29.7 %reduce-scatter.10.cloned.1.call-done = f32[512,256]{1,0:T(8,128)} async-done(((f32[2048,256]{1,0:T(8,128)}), f32[512,256]{1,0:T(8,128)}) %reduce-scatter.10.cloned.1.call-update) | async-done | bytes 524304 | tf_op jit(solution)/shard_map/reduce_scatter | solution.py:63
  1086.0 252.2 %all-reduce.11.cloned.1.call-done = f32[256,256]{0,1:T(8,128)} async-done(((f32[256,256]{0,1:T(8,128)}), f32[256,256]{0,1:T(8,128)}) %all-reduce.11.cloned.1.call-update) | async-done | bytes 262160 | tf_op jit(solution)/shard_map/psum | solution.py:64
  1340.4 11.7 cholesky.324
  1352.2 9.8 custom-call.23
  1362.5 11.7 cholesky.341
  1377.0 4.5 while.12
  1381.5 19.7 custom-call.24
  1403.5 25.8 %all-gather.12.cloned.1.call-done = bf16[2048,256]{1,0:T(8,128)(2,1)} async-done(((bf16[512,256]{1,0:T(8,128)(2,1)}), bf16[2048,256]{1,0:T(8,128)(2,1)}) %all-gather.12.cloned.1.call-update) | async-done | bytes 1048592 | tf_op jit(solution)/shard_map/all_gather | solution.py:68
  1433.9 5.5 copy.40
  1445.8 136.9 %reduce-scatter.12.cloned.1.call-done = f32[32,256]{1,0:T(8,128)} async-done(((f32[2048,256]{1,0:T(8,128)}), f32[32,256]{1,0:T(8,128)}) %reduce-scatter.12.cloned.1.call-update) | async-done | bytes 32784 | tf_op jit(solution)/shard_map/reduce_scatter | solution.py:77
  1584.9 256.0 %all-reduce.13.cloned.1.call-done = f32[256,256]{0,1:T(8,128)} async-done(((f32[256,256]{0,1:T(8,128)}), f32[256,256]{0,1:T(8,128)}) %all-reduce.13.cloned.1.call-update) | async-done | bytes 262160 | tf_op jit(solution)/shard_map/psum | solution.py:80
  1843.0 11.7 cholesky.358
  1854.7 9.8 custom-call.25
  1865.0 11.7 cholesky.375
  1879.5 4.3 while.13
  1883.9 19.7 custom-call.26
  1905.5 76.9 %all-gather.16.cloned.1.call-done = bf16[2048,256]{1,0:T(8,128)(2,1)} async-done(((bf16[32,256]{1,0:T(8,128)(2,1)}), bf16[2048,256]{1,0:T(8,128)(2,1)}) %all-gather.16.cloned.1.call-update) | async-done | bytes 1048592 | tf_op jit(solution)/shard_map/all_gather | solution.py:61
  1987.0 5.5 copy.42
  1999.2 29.5 %reduce-scatter.14.cloned.1.call-done = f32[512,256]{1,0:T(8,128)} async-done(((f32[2048,256]{1,0:T(8,128)}), f32[512,256]{1,0:T(8,128)}) %reduce-scatter.14.cloned.1.call-update) | async-done | bytes 524304 | tf_op jit(solution)/shard_map/reduce_scatter | solution.py:63
  2031.6 252.5 %all-reduce.15.cloned.1.call-done = f32[256,256]{0,1:T(8,128)} async-done(((f32[256,256]{0,1:T(8,128)}), f32[256,256]{0,1:T(8,128)}) %all-reduce.15.cloned.1.call-update) | async-done | bytes 262160 | tf_op jit(solution)/shard_map/psum | solution.py:64
  2286.2 11.7 cholesky.392
  2297.9 9.8 custom-call.27
  2308.2 11.7 cholesky.409
  2322.7 4.4 while.14
  2327.2 19.7 custom-call.28
  (191 shorter events, 110.7 us)
Async XLA Ops:
  7.2 86.1 %copy-start = (bf16[1,1,32,128,128]{4,3,2,1,0:T(8,128)(2,1)S(1)}, bf16[1,1,32,128,128]{4,3,2,1,0:T(8,128)(2,1)}, u32[]{:S(2)}) copy-start(bf16[1,1,32,128,128]{4,3,2,1,0:T(8,128)(2,1)} %param.8) | copy-start | bytes 3145732
  7.2 84.2 %all-gather.8.cloned.1.call-start = ((), (), s32[]{:S(2)}) async-start(), calls=%async_computation.5 | async-start | bytes 1064960 | tf_op jit(solution)/shard_map/all_gather | solution.py:61
  7.9 129.7 %reduce-scatter.6.cloned.1.call-start = ((), (), s32[]{:S(2)}) async-start(), calls=%async_computation.6 | async-start | bytes 2621440 | tf_op jit(solution)/shard_map/reduce_scatter | solution.py:63
  96.0 5.5 copy-start.6
  107.9 285.3 %all-reduce.7.cloned.1.call-start = ((), (), s32[]{:S(2)}) async-start(), calls=%async_computation.7 | async-start | bytes 524288 | tf_op jit(solution)/shard_map/psum | solution.py:64
  140.5 343.0 %all-gather.10.cloned.1.call-start = ((), (), s32[]{:S(2)}) async-start(), calls=%async_computation.8 | async-start | bytes 1310720 | tf_op jit(solution)/shard_map/all_gather | solution.py:68
  395.3 61.0 %copy-start.1 = (f32[512,256]{1,0:T(8,128)S(1)}, f32[512,256]{1,0:T(8,128)}, u32[]{:S(2)}) copy-start(f32[512,256]{1,0:T(8,128)} %reduce-scatter.6.cloned.1.call-done) | copy-start | bytes 1572868
  457.6 179.3 %reduce-scatter.8.cloned.1.call-start = ((), (), s32[]{:S(2)}) async-start(), calls=%async_computation.9 | async-start | bytes 2129920 | tf_op jit(solution)/shard_map/reduce_scatter | solution.py:77
  488.1 5.5 copy-start.7
  500.0 395.1 %all-reduce.9.cloned.1.call-start = ((), (), s32[]{:S(2)}) async-start(), calls=%async_computation.10 | async-start | bytes 524288 | tf_op jit(solution)/shard_map/psum | solution.py:80
  638.9 397.7 %all-gather.14.cloned.1.call-start = ((), (), s32[]{:S(2)}) async-start(), calls=%async_computation.18 | async-start | bytes 1064960 | tf_op jit(solution)/shard_map/all_gather | solution.py:61
  897.2 61.5 %copy-start.4 = (f32[32,256]{1,0:T(8,128)S(1)}, f32[32,256]{1,0:T(8,128)}, u32[]{:S(2)}) copy-start(f32[32,256]{1,0:T(8,128)} %reduce-scatter.8.cloned.1.call-done) | copy-start | bytes 98308
  959.6 123.2 %reduce-scatter.10.cloned.1.call-start = ((), (), s32[]{:S(2)}) async-start(), calls=%async_computation.11 | async-start | bytes 2621440 | tf_op jit(solution)/shard_map/reduce_scatter | solution.py:63
  1053.1 285.2 %all-reduce.11.cloned.1.call-start = ((), (), s32[]{:S(2)}) async-start(), calls=%async_computation.12 | async-start | bytes 524288 | tf_op jit(solution)/shard_map/psum | solution.py:64
  1085.8 343.5 %all-gather.12.cloned.1.call-start = ((), (), s32[]{:S(2)}) async-start(), calls=%async_computation.13 | async-start | bytes 1310720 | tf_op jit(solution)/shard_map/all_gather | solution.py:68
  1340.4 61.7 %copy-start.3 = (f32[512,256]{1,0:T(8,128)S(1)}, f32[512,256]{1,0:T(8,128)}, u32[]{:S(2)}) copy-start(f32[512,256]{1,0:T(8,128)} %reduce-scatter.10.cloned.1.call-done) | copy-start | bytes 1572868
  1403.4 179.3 %reduce-scatter.12.cloned.1.call-start = ((), (), s32[]{:S(2)}) async-start(), calls=%async_computation.14 | async-start | bytes 2129920 | tf_op jit(solution)/shard_map/reduce_scatter | solution.py:77
  1445.8 395.1 %all-reduce.13.cloned.1.call-start = ((), (), s32[]{:S(2)}) async-start(), calls=%async_computation.15 | async-start | bytes 524288 | tf_op jit(solution)/shard_map/psum | solution.py:80
  1584.7 397.7 %all-gather.16.cloned.1.call-start = ((), (), s32[]{:S(2)}) async-start(), calls=%async_computation.19 | async-start | bytes 1064960 | tf_op jit(solution)/shard_map/all_gather | solution.py:61
  1842.9 61.5 %copy-start.5 = (f32[32,256]{1,0:T(8,128)S(1)}, f32[32,256]{1,0:T(8,128)}, u32[]{:S(2)}) copy-start(f32[32,256]{1,0:T(8,128)} %reduce-scatter.12.cloned.1.call-done) | copy-start | bytes 98308
  1905.4 123.2 %reduce-scatter.14.cloned.1.call-start = ((), (), s32[]{:S(2)}) async-start(), calls=%async_computation.16 | async-start | bytes 2621440 | tf_op jit(solution)/shard_map/reduce_scatter | solution.py:63
  1998.9 285.2 %all-reduce.15.cloned.1.call-start = ((), (), s32[]{:S(2)}) async-start(), calls=%async_computation.17 | async-start | bytes 524288 | tf_op jit(solution)/shard_map/psum | solution.py:64
  2297.9 50.6 %copy-start.2 = (f32[512,256]{1,0:T(8,128)S(1)}, f32[512,256]{1,0:T(8,128)}, u32[]{:S(2)}) copy-start(f32[512,256]{1,0:T(8,128)} %reduce-scatter.14.cloned.1.call-done) | copy-start | bytes 1572868
Sparse Core Ops, SparseCore 0:
  10.8 80.5 all-gather.7
  108.0 29.5 reduce-scatter.5
  144.5 248.5 all-reduce.6
  457.7 25.7 all-gather.9
  500.1 136.7 reduce-scatter.7
  642.8 252.2 all-reduce.8
  959.7 76.8 all-gather.13
  1053.2 29.6 reduce-scatter.9
  1089.8 248.4 all-reduce.10
  1403.5 25.7 all-gather.11
  1445.9 136.7 reduce-scatter.11
  1588.6 252.2 all-reduce.12
  1905.6 76.8 all-gather.15
  1999.0 29.5 reduce-scatter.13
  2035.4 248.5 all-reduce.14
where the time goes:
time: 2360 us
  waiting for transfers between devices  1920 us (81%)
  other arithmetic  282 us (12%)
  local copies, waits for them, and re-layouts  71.9 us (3%)
  matrix products  57.6 us (2%)
    psum x3, waiting for transfers between devices, row_side(): gram = lax.psum(inner_gram(shares), ('rows', 'cols'))  757 us
    psum x2, waiting for transfers between devices, shards(): column_gram = lax.psum(inner_gram(column_shares), ('rows', 'cols'))  512 us
    reduce_scatter x2, waiting for transfers between devices, shards(): lax.psum_scatter(column_partial_value, 'rows', scatter_dimension=0, tiled...  274 us
    all_gather x3, waiting for transfers between devices, row_side(): xgroup = lax.all_gather(xpiece, 'rows', axis=1, tiled=True)[0]  236 us
    another operation x34, other arithmetic, lower_factor(): lower = jnp.linalg.cholesky(gram)  173 us
    another operation x10, other arithmetic, lower_factor(): jax.scipy.linalg.solve_triangular(lower, jnp.eye(gram.shape[0], dtype=jnp...  98.5 us
    reduce_scatter x3, waiting for transfers between devices, row_side(): lax.psum_scatter(partial_value, 'cols', scatter_dimension=0, tiled=True)  88.9 us
    all_gather x2, waiting for transfers between devices, row_side(): lax.all_gather(mine.astype(jnp.bfloat16), 'cols', axis=0, tiled=True)  51.7 us
  transfers between devices with their start and end apart: 15, of which 15 were waited for; matrix products, arithmetic and copies ran while one was open for 0% of the time, Pallas kernels for 0%

commit v1 on v0

v1 whole, which is shorter than its diff:
```python
import functools

import jax
import jax.numpy as jnp
from jax import lax
from jax.experimental import pallas as pl
from jax.experimental.pallas import tpu as pltpu
from jax.sharding import PartitionSpec as P

ROUNDS = 2
TR = 16
CGT = 16
TILE = 128
K = 256
SLOTS = 32
NZ = 8
NX = 4
NY = 4
PANEL = 64
COPIES = 80
F32 = jnp.float32
BF16 = jnp.bfloat16
HI = lax.Precision.HIGHEST
MESH = pl.DeviceIdType.MESH
VM = pltpu.VMEM
MIB = 1024 * 1024


def order_kernel(rows_ref, cols_ref, count_ref, byrow_ref, bycol_ref, cnt_ref):
    live = count_ref[0]

    def one(key_ref, other_ref, out_ref):
        for b in range(TR + 1):
            cnt_ref[b] = 0

        def count(t, carry):
            b = jnp.where(t < live, key_ref[t], TR)
            cnt_ref[b] = cnt_ref[b] + 1
            return carry

        lax.fori_loop(0, SLOTS, count, 0)
        at = jnp.int32(0)
        for b in range(TR + 1):
            n = cnt_ref[b]
            cnt_ref[b] = at
            if b < TR:
                out_ref[112 + b] = jnp.where(n > 0, 1, 0)
                out_ref[96 + b] = jnp.maximum(at + n - 1, 0)
            at = at + n

        def clear(t, carry):
            out_ref[64 + t] = 1
            return carry

        lax.fori_loop(0, SLOTS, clear, 0)
        for b in range(TR + 1):
            first = cnt_ref[b]

            @pl.when(first < SLOTS)
            def _():
                out_ref[64 + first] = 0

        def place(t, carry):
            b = jnp.where(t < live, key_ref[t], TR)
            k = cnt_ref[b]
            cnt_ref[b] = k + 1
            out_ref[k] = t
            out_ref[32 + k] = other_ref[t]
            return carry

        lax.fori_loop(0, SLOTS, place, 0)

    one(rows_ref, cols_ref, byrow_ref)
    one(cols_ref, rows_ref, bycol_ref)


def slot_orders(rows_idx, cols_idx, count):
    smem = pl.BlockSpec(memory_space=pltpu.SMEM)
    out = jax.ShapeDtypeStruct((128,), jnp.int32)
    return pl.pallas_call(
        order_kernel,
        name="orders",
        out_shape=(out, out),
        in_specs=[smem] * 3,
        out_specs=[smem] * 2,
        scratch_shapes=[pltpu.SMEM((TR + 1,), jnp.int32)],
    )(rows_idx, cols_idx, count)


def factor_kernel(scale, last, *refs):
    if last:
        g_ref, y_ref, q_ref, u_ref, x_ref, a_ref, e_ref = refs
    else:
        g_ref, x_ref, u_ref, a_ref, e_ref = refs
    n = K
    dn = (((0,), (0,)), ((), ()))
    a_ref[...] = g_ref[...] * scale
    row_i = lax.broadcasted_iota(jnp.int32, (n, n), 0)
    col_i = lax.broadcasted_iota(jnp.int32, (n, n), 1)
    e_ref[...] = jnp.where(row_i == col_i, 1.0, 0.0)
    sub = lax.broadcasted_iota(jnp.int32, (PANEL, 1), 0)
    for k in range(n // PANEL):
        lo = k * PANEL
        r = a_ref[lo : lo + PANEL, :]
        e = e_ref[lo : lo + PANEL, :]
        for j in range(PANEL):
            c = lo + j
            inv = lax.rsqrt(r[j : j + 1, c : c + 1])
            urow = r[j : j + 1, :] * inv
            xrow = e[j : j + 1, :] * inv
            f = jnp.where(sub > j, r[:, c : c + 1] * inv, 0.0)
            r = r - f * urow
            e = e - f * xrow
            u_ref[c : c + 1, :] = urow
            x_ref[c : c + 1, :] = xrow
        if lo + PANEL < n:
            u = u_ref[lo : lo + PANEL, :]
            x = x_ref[lo : lo + PANEL, :]
            a_ref[...] -= lax.dot_general(u, u, dn, precision=HI, preferred_element_type=F32)
            e_ref[...] -= lax.dot_general(u, x, dn, precision=HI, preferred_element_type=F32)
    if last:
        u_ref[...] = jnp.where(col_i >= row_i, u_ref[...], 0.0)
        q_ref[...] = apply_inverse(y_ref[...], x_ref[...])


def apply_inverse(share, inverse):
    return lax.dot_general(
        share, inverse, (((1,), (1,)), ((), ())), precision=HI, preferred_element_type=F32
    )


def factorize(gram, scale, share=None):
    vmem = pl.BlockSpec(memory_space=VM)
    square = jax.ShapeDtypeStruct((K, K), F32)
    buf = pltpu.VMEM((K, K), F32)
    params = pltpu.CompilerParams(vmem_limit_bytes=32 * MIB)
    if share is None:
        return pl.pallas_call(
            functools.partial(factor_kernel, scale, False),
            name="factor",
            out_shape=square,
            in_specs=[vmem],
            out_specs=vmem,
            scratch_shapes=[buf] * 3,
            compiler_params=params,
        )(gram)
    return pl.pallas_call(
        functools.partial(factor_kernel, scale, True),
        name="factor_apply",
        out_shape=(jax.ShapeDtypeStruct(share.shape, F32), square),
        in_specs=[vmem] * 2,
        out_specs=[vmem] * 2,
        scratch_shapes=[buf] * 3,
        compiler_params=params,
    )(gram, share)


class Net:
    def __init__(self, send, recv):
        self.send, self.recv, self.copies = send, recv, []

    def start(self, src, dst, device):
        k = len(self.copies)
        copy = pltpu.make_async_remote_copy(
            src_ref=src,
            dst_ref=dst,
            send_sem=self.send.at[k],
            recv_sem=self.recv.at[k],
            device_id=device,
            device_id_type=MESH,
        )
        copy.start()
        self.copies.append(copy)
        return copy

    def drain(self):
        for copy in self.copies:
            copy.wait_send()


def ring4(me):
    return lax.rem(me + 1, 4), lax.rem(me + 3, 4), lax.rem(me + 2, 4)


def gather4(net, loc, me, to, arrived=None):
    right, left, opp = ring4(me)
    r_a = net.start(loc(me, 0), loc(me, 0), to(right))
    l_b = net.start(loc(me, 1), loc(me, 1), to(left))
    r_b = net.start(loc(me, 1), loc(me, 1), to(right))
    l_a = net.start(loc(me, 0), loc(me, 0), to(left))
    if arrived is not None:
        arrived(me)
    r_a.wait_recv()
    f_a = net.start(loc(left, 0), loc(left, 0), to(right))
    l_b.wait_recv()
    f_b = net.start(loc(right, 1), loc(right, 1), to(left))
    r_b.wait_recv()
    if arrived is not None:
        arrived(left)
    l_a.wait_recv()
    if arrived is not None:
        arrived(right)
    f_a.wait_recv()
    f_b.wait_recv()
    if arrived is not None:
        arrived(opp)


def scatter4(net, src, me, to, buf, tmp, store, ready=None):
    right, left, opp = ring4(me)
    if ready is None:
        ready = lambda p: None
    ready(opp)
    a0 = net.start(src(opp, 0), buf.at[0], to(right))
    b0 = net.start(src(opp, 1), buf.at[1], to(left))
    ready(right)
    b1 = net.start(src(right, 1), buf.at[2], to(right))
    ready(left)
    a1 = net.start(src(left, 0), buf.at[3], to(left))
    a0.wait_recv()
    tmp[0] = src(right, 0)[...] + buf[0]
    a2 = net.start(tmp.at[0], buf.at[4], to(right))
    b0.wait_recv()
    tmp[1] = src(left, 1)[...] + buf[1]
    b2 = net.start(tmp.at[1], buf.at[5], to(left))
    ready(me)
    a1.wait_recv()
    b1.wait_recv()
    a2.wait_recv()
    store(0, src(me, 0)[...] + (buf[3] + buf[4]))
    b2.wait_recv()
    store(1, src(me, 1)[...] + (buf[2] + buf[5]))


def tile_products(tiles_ref, order_ref, load, prefix_ref, store, transposed):
    dn = (((0,), (0,)), ((), ())) if transposed else (((1,), (0,)), ((), ()))

    def step(k, acc):
        prod = lax.dot_general(
            tiles_ref[order_ref[k]], load(order_ref[32 + k]), dn, preferred_element_type=F32
        )
        acc = acc * order_ref[64 + k].astype(F32) + prod
        prefix_ref[k] = acc
        return acc

    lax.fori_loop(0, SLOTS, step, jnp.zeros((TILE, K), F32), unroll=4)
    for b in range(TR):
        store(b, prefix_ref[order_ref[96 + b]] * order_ref[112 + b].astype(F32))


def half_kernel(kind, *refs):
    if kind == "first":
        piece_ref, refs = refs[0], refs[1:]
    else:
        piece_ref, inverse_ref, refs = refs[0], refs[1], refs[2:]
    tiles_ref, order_ref, share_ref, gram_ref = refs[:4]
    x_ref, prefix_ref, part_ref = refs[4:7]
    g_ref, g1_ref, s1_ref, g2_ref, s2_ref, g3_ref, gf_ref = refs[7:14]
    send, recv = refs[14:16]
    buf_ref, tmp_ref = refs[16:18]
    transposed = kind == "columns"
    if transposed:
        r0_ref, c1_ref, c2_ref, rz_ref = refs[18:22]

    row, y = lax.axis_index("rows"), lax.axis_index("cols")
    core = lax.rem(row, 2)
    x = lax.rem(lax.div(row, 2), NX)
    z = lax.div(row, 2 * NX)
    q = lax.rem(row, 2 * NX)
    net = Net(send, recv)

    def at(z_, q_, y_):
        return (z_ * (2 * NX) + q_, y_)

    to_z = lambda p: at(p, q, y)
    to_q = lambda p: at(z, p, y)
    to_x = lambda p: at(z, p * 2 + core, y)
    to_y = lambda p: at(z, q, p)
    other_core = at(z, x * 2 + (1 - core), y)

    barrier = pltpu.get_barrier_semaphore()
    for d in range(1, NZ):
        pl.semaphore_signal(barrier, 1, device_id=to_z(lax.rem(z + d, NZ)), device_id_type=MESH)
    for d in range(1, 2 * NX):
        pl.semaphore_signal(barrier, 1, device_id=to_q(lax.rem(q + d, 2 * NX)), device_id_type=MESH)
    for d in range(1, NY):
        pl.semaphore_signal(barrier, 1, device_id=to_y(lax.rem(y + d, NY)), device_id_type=MESH)
    pl.semaphore_wait(barrier, NZ - 1 + 2 * NX - 1 + NY - 1)

    if transposed:
        mine = apply_inverse(piece_ref[...], inverse_ref[...]).astype(BF16)
        x_ref[y] = mine.reshape(2, 2, TILE, K)
        gather4(net, lambda p, h: x_ref.at[p, h], y, to_y)

        def load(b):
            return x_ref[b >> 2, (b >> 1) & 1, b & 1]

    else:
        xh, xl = lax.div(x, 2), lax.rem(x, 2)
        if kind == "first":
            x_ref[z, xh, xl, core] = piece_ref[...]
        else:
            x_ref[z, xh, xl, core] = apply_inverse(piece_ref[...], inverse_ref[...]).astype(BF16)
        spot = x_ref.at[z, xh, xl, core]
        copies = [net.start(spot, spot, to_z(lax.rem(z + d, NZ))) for d in range(1, NZ)]
        for copy in copies:
            copy.wait_recv()
        crossing = []

        def cross(p):
            spot = x_ref.at[:, lax.div(p, 2), lax.rem(p, 2), core]
            crossing.append(net.start(spot, spot, other_core))

        gather4(
            net,
            lambda p, h: x_ref.at[pl.ds(h * (NZ // 2), NZ // 2), lax.div(p, 2), lax.rem(p, 2), core],
            x,
            to_x,
            cross,
        )
        for copy in crossing:
            copy.wait_recv()

        def load(b):
            return x_ref[b >> 1, b & 1].reshape(TILE, K)

    if transposed:
        def keep(b, value):
            part_ref[b // 2, b % 2] = value.reshape(2, 2, 32, K)

        tile_products(tiles_ref, order_ref, load, prefix_ref, keep, True)
        right, left, opp = ring4(x)
        crossed = {}
        for name, p in (("opp", opp), ("right", right), ("left", left), ("me", x)):
            src = part_ref.at[:, lax.div(p, 2), lax.rem(p, 2), 1 - core]
            crossed[name] = net.start(src, r0_ref.at[p], other_core)
        names = iter(("opp", "right", "left", "me"))

        def ready(p):
            crossed[next(names)].wait_recv()
            c1_ref[p] = part_ref[:, lax.div(p, 2), lax.rem(p, 2), core] + r0_ref[p]

        def store(h, value):
            c2_ref[pl.ds(h * (NZ // 2), NZ // 2)] = value

        scatter4(
            net,
            lambda p, h: c1_ref.at[p, pl.ds(h * (NZ // 2), NZ // 2)],
            x,
            to_x,
            buf_ref,
            tmp_ref,
            store,
            ready,
        )
        copies = []
        for d in range(1, NZ):
            p = lax.rem(z + d, NZ)
            copies.append(net.start(c2_ref.at[p], rz_ref.at[d - 1], to_z(p)))
        total = c2_ref[z]
        for d, copy in enumerate(copies):
            copy.wait_recv()
            total = total + rz_ref[d]
        share = total
    else:
        def keep(b, value):
            part_ref[b // 4, (b // 2) % 2, b % 2] = value

        tile_products(tiles_ref, order_ref, load, prefix_ref, keep, False)

        def store(h, value):
            share_ref[h * 2 * TILE : (h + 1) * 2 * TILE, :] = value.reshape(2 * TILE, K)

        scatter4(
            net, lambda p, h: part_ref.at[p, h], y, to_y, buf_ref, tmp_ref, store
        )
        share = share_ref[...]
    if transposed:
        share_ref[...] = share

    gram = lax.dot_general(
        share, share, (((0,), (0,)), ((), ())), precision=HI, preferred_element_type=F32
    )
    g_ref[0] = gram[:, :128]
    g_ref[1] = gram[:, 128:]
    wide, thin = K // NX, K // NX // NZ
    copies = []
    for d in range(1, 2 * NX):
        p = lax.rem(q + d, 2 * NX)
        src = g_ref.at[lax.rem(p, 2), pl.ds(pl.multiple_of(lax.div(p, 2) * wide, wide), wide)]
        copies.append(net.start(src, g1_ref.at[d - 1], to_q(p)))
    total = g_ref[core, pl.ds(pl.multiple_of(x * wide, wide), wide)]
    for d, copy in enumerate(copies):
        copy.wait_recv()
        total = total + g1_ref[d]
    s1_ref[...] = total
    copies = []
    for d in range(1, NZ):
        p = lax.rem(z + d, NZ)
        src = s1_ref.at[pl.ds(pl.multiple_of(p * thin, thin), thin)]
        copies.append(net.start(src, g2_ref.at[d - 1], to_z(p)))
    total = s1_ref[pl.ds(pl.multiple_of(z * thin, thin), thin)]
    for d, copy in enumerate(copies):
        copy.wait_recv()
        total = total + g2_ref[d]
    g3_ref[y] = total
    copies = [
        net.start(g3_ref.at[y], g3_ref.at[y], to_y(lax.rem(y + d, NY))) for d in range(1, NY)
    ]
    for copy in copies:
        copy.wait_recv()
    total = (g3_ref[0] + g3_ref[1]) + (g3_ref[2] + g3_ref[3])
    at_thin = pl.ds(pl.multiple_of(x * wide + z * thin, thin), thin)
    gf_ref[core, at_thin] = total
    spot = gf_ref.at[core, at_thin]
    copies = [net.start(spot, spot, to_z(lax.rem(z + d, NZ))) for d in range(1, NZ)]
    for copy in copies:
        copy.wait_recv()
    spot = gf_ref.at[core, pl.ds(pl.multiple_of(x * wide, wide), wide)]
    copies = [net.start(spot, spot, to_q(lax.rem(q + d, 2 * NX))) for d in range(1, 2 * NX)]
    for copy in copies:
        copy.wait_recv()
    gram_ref[:, :128] = gf_ref[0]
    gram_ref[:, 128:] = gf_ref[1]
    net.drain()


COLLECTIVE = {"first": 1, "columns": 2, "rows": 3}


def half_round(kind, piece, inverse, tiles, order):
    transposed = kind == "columns"
    by_y = (NY, 2, 2, TILE, K)
    by_row = (NZ, 2, 2, 2, 32, K)
    share = (32, K) if transposed else (4 * TILE, K)
    half = (NZ // 2, 32, K) if transposed else (2, TILE, K)
    wide, thin = K // NX, K // NX // NZ
    scratch = [
        VM(by_y if transposed else by_row, BF16),
        VM((SLOTS, TILE, K), F32),
        VM(by_row if transposed else by_y, F32),
        VM((2, K, 128), F32),
        VM((2 * NX - 1, wide, 128), F32),
        VM((wide, 128), F32),
        VM((NZ - 1, thin, 128), F32),
        VM((thin, 128), F32),
        VM((NY, thin, 128), F32),
        VM((2, K, 128), F32),
        pltpu.SemaphoreType.DMA((COPIES,)),
        pltpu.SemaphoreType.DMA((COPIES,)),
        VM((6,) + half, F32),
        VM((2,) + half, F32),
    ]
    if transposed:
        scratch += [
            VM((NX, NZ, 32, K), F32),
            VM((NX, NZ, 32, K), F32),
            VM((NZ, 32, K), F32),
            VM((NZ - 1, 32, K), F32),
        ]
    operands = [piece] + ([] if inverse is None else [inverse]) + [tiles, order]
    vmem = pl.BlockSpec(memory_space=VM)
    return pl.pallas_call(
        functools.partial(half_kernel, kind),
        name="half_" + kind,
        out_shape=(jax.ShapeDtypeStruct(share, F32), jax.ShapeDtypeStruct((K, K), F32)),
        in_specs=[vmem] * (len(operands) - 1) + [pl.BlockSpec(memory_space=pltpu.SMEM)],
        out_specs=[vmem] * 2,
        scratch_shapes=scratch,
        compiler_params=pltpu.CompilerParams(
            collective_id=COLLECTIVE[kind], has_side_effects=True, vmem_limit_bytes=48 * MIB
        ),
    )(*operands)


def shards(tiles, tile_rows, tile_cols, tile_counts, sketch):
    blocks = tiles[0, 0]
    total_rows = TR * TILE * lax.axis_size("rows")
    total_cols = CGT * TILE * lax.axis_size("cols")
    by_row, by_col = slot_orders(tile_rows[0, 0], tile_cols[0, 0], tile_counts[0])
    share, gram = half_round("first", sketch[0], None, blocks, by_row)
    for step in range(ROUNDS):
        inverse = factorize(gram, 1.0 / total_rows)
        share, gram = half_round("columns", share, inverse, blocks, by_col)
        inverse = factorize(gram, 1.0 / total_cols)
        share, gram = half_round("rows", share, inverse, blocks, by_row)
    return factorize(gram, 1.0 / total_rows, share)


def solution(mesh):
    return jax.shard_map(
        shards,
        mesh=mesh,
        in_specs=(
            P("rows", "cols", None, None, None),
            P("rows", "cols", None),
            P("rows", "cols", None),
            P("rows", "cols"),
            P("cols", "rows", None),
        ),
        out_specs=(P(("rows", "cols"), None), P()),
        check_vma=False,
    )
```

time: 2360 us -> 454 us (0.19)
  waiting for transfers between devices: 1920 us -> 0 us
  Pallas kernels: 0 us -> 443 us
  other arithmetic: 282 us -> 0 us
  local copies, waits for them, and re-layouts: 71.9 us -> 1.88 us
  matrix products: 57.6 us -> 0 us
    psum x5 -> x0, waiting for transfers between devices: 1270 us -> none  [the longest x3 757 us: row_side(): gram = lax.psum(inner_gram(shares), ('rows', 'cols'))]
    pallas_call x0 -> x11, Pallas kernels: none -> 443 us  [the longest x5 324 us: half_round(): pl.pallas_call(functools.partial(half_kernel, kind), name='half_' + kind,...]
    reduce_scatter x5 -> x0, waiting for transfers between devices: 363 us -> none  [the longest x2 274 us: shards(): lax.psum_scatter(column_partial_value, 'rows', scatter_dimension=0, tiled...]
    all_gather x5 -> x0, waiting for transfers between devices: 288 us -> none  [the longest x3 236 us: row_side(): xgroup = lax.all_gather(xpiece, 'rows', axis=1, tiled=True)[0]]
    another operation x44 -> x0, other arithmetic: 271 us -> none  [the longest x34 173 us: lower_factor(): lower = jnp.linalg.cholesky(gram)]
    dot_general x20 -> x0, matrix products: 50.9 us -> none  [the longest x5 12.6 us: inner_gram(): return jnp.dot(matrix.T, matrix, precision=lax.Precision.HIGHEST)]
    dot_general x10 -> x0, local copies, waits for them, and re-layouts: 40.4 us -> none  [the longest x3 16.5 us: tile_product(): jnp.einsum('tij,tjk->tik', blocks, picked, preferred_element_type=jnp.flo...]
  transfers between devices with their start and end apart: 15 -> 0, of which waited for: 15 -> 0; matrix products, arithmetic and copies ran while one was open for 0% -> 0% of each run, Pallas kernels for 0% -> 0%
where the time goes in v1:
time: 454 us; the launch traced here: 446 us
  Pallas kernels  443 us (98%)
    pallas_call x5, Pallas kernels, half_round(): pl.pallas_call(functools.partial(half_kernel, kind), name='half_' + kind,...  324 us
    pallas_call x4, Pallas kernels, factorize(): pl.pallas_call(functools.partial(factor_kernel, scale, False), name='fact...  91.6 us
    pallas_call x1, Pallas kernels, factorize(): pl.pallas_call(functools.partial(factor_kernel, scale, True), name='facto...  24.3 us

profile of v1, /device:TPU:1, one launch (start us, length us, event | category | flops | bytes accessed | tf_op | source)
XLA Modules:
  0.0 446.3 jit_solution(3455414227710339683)
XLA Ops:
  0.6 0.0 copy-start.2
  1.3 3.1 orders.1
  4.4 0.0 copy-start.3
  4.4 0.0 copy-done.2
  4.4 0.6 copy-done.3
  5.0 0.0 copy-start
  5.0 1.2 copy-done
  6.3 0.0 copy-start.1
  6.3 69.9 %half_first.1 = (f32[512,256]{1,0:T(8,128)S(1)}, f32[256,256]{1,0:T(8,128)S(1)}) custom-call(bf16[32,256]{1,0:T(8,128)(2,1)S(1)} %bitcast.11, bf16[32,128,128]{2,1,0:T(8,128)(2,1)S(1)} %bitcast.6, s32[128]{0:T(128)S(1)} %copy-done.3), custom_call_target="tpu_custom_call" | custom-call | tf_op jit(solution)/shard_map/half_first/pallas_call | solution.py:463
  76.2 0.0 copy-start.4
  76.2 22.9 %factor.4.refs_1_ = f32[256,256]{1,0:T(8,128)S(1)} custom-call(f32[256,256]{1,0:T(8,128)S(1)} %get-tuple-element.16.refs_0_), custom_call_target="tpu_custom_call" | custom-call | tf_op jit(solution)/shard_map/factor/pallas_call | solution.py:138
  99.1 0.0 copy-done.1
  99.1 0.0 copy-done.4
  99.1 62.0 %half_columns.2 = (f32[32,256]{1,0:T(8,128)S(1)}, f32[256,256]{1,0:T(8,128)S(1)}) custom-call(f32[512,256]{1,0:T(8,128)S(1)} %get-tuple-element.15.refs_0_, f32[256,256]{1,0:T(8,128)S(1)} %factor.4.refs_1_, bf16[32,128,128]{2,1,0:T(8,128)(2,1)S(1)} %bitcast.7, s32[128]{0:T(128)S(1)} %copy-done.4), custom_call_target="tpu_custom_call" | custom-call | tf_op jit(solution)/shard_map/half_columns/pallas_call | solution.py:463
  161.2 22.9 %factor.5.refs_1_ = f32[256,256]{1,0:T(8,128)S(1)} custom-call(f32[256,256]{1,0:T(8,128)S(1)} %get-tuple-element.19.refs_0_), custom_call_target="tpu_custom_call" | custom-call | tf_op jit(solution)/shard_map/factor/pallas_call | solution.py:138
  184.1 64.7 %half_rows.2 = (f32[512,256]{1,0:T(8,128)S(1)}, f32[256,256]{1,0:T(8,128)S(1)}) custom-call(f32[32,256]{1,0:T(8,128)S(1)} %get-tuple-element.18.refs_0_, f32[256,256]{1,0:T(8,128)S(1)} %factor.5.refs_1_, bf16[32,128,128]{2,1,0:T(8,128)(2,1)S(1)} %bitcast.8, s32[128]{0:T(128)S(1)} %copy-done.3), custom_call_target="tpu_custom_call" | custom-call | tf_op jit(solution)/shard_map/half_rows/pallas_call | solution.py:463
  248.8 22.9 %factor.6.refs_1_ = f32[256,256]{1,0:T(8,128)S(1)} custom-call(f32[256,256]{1,0:T(8,128)S(1)} %get-tuple-element.21.refs_0_), custom_call_target="tpu_custom_call" | custom-call | tf_op jit(solution)/shard_map/factor/pallas_call | solution.py:138
  271.8 62.4 %half_columns.3 = (f32[32,256]{1,0:T(8,128)S(1)}, f32[256,256]{1,0:T(8,128)S(1)}) custom-call(f32[512,256]{1,0:T(8,128)S(1)} %get-tuple-element.20.refs_0_, f32[256,256]{1,0:T(8,128)S(1)} %factor.6.refs_1_, bf16[32,128,128]{2,1,0:T(8,128)(2,1)S(1)} %bitcast.9, s32[128]{0:T(128)S(1)} %copy-done.4), custom_call_target="tpu_custom_call" | custom-call | tf_op jit(solution)/shard_map/half_columns/pallas_call | solution.py:463
  334.1 22.9 %factor.7.refs_1_ = f32[256,256]{1,0:T(8,128)S(1)} custom-call(f32[256,256]{1,0:T(8,128)S(1)} %get-tuple-element.23.refs_0_), custom_call_target="tpu_custom_call" | custom-call | tf_op jit(solution)/shard_map/factor/pallas_call | solution.py:138
  357.0 64.7 %half_rows.3 = (f32[512,256]{1,0:T(8,128)S(1)}, f32[256,256]{1,0:T(8,128)S(1)}) custom-call(f32[32,256]{1,0:T(8,128)S(1)} %get-tuple-element.22.refs_0_, f32[256,256]{1,0:T(8,128)S(1)} %factor.7.refs_1_, bf16[32,128,128]{2,1,0:T(8,128)(2,1)S(1)} %bitcast.10, s32[128]{0:T(128)S(1)} %copy-done.3), custom_call_target="tpu_custom_call" | custom-call | tf_op jit(solution)/shard_map/half_rows/pallas_call | solution.py:463
  421.8 24.3 %factor_apply.1 = (f32[512,256]{1,0:T(8,128)}, f32[256,256]{1,0:T(8,128)}) custom-call(f32[256,256]{1,0:T(8,128)S(1)} %get-tuple-element.24.refs_0_, f32[512,256]{1,0:T(8,128)S(1)} %get-tuple-element.25.refs_1_), custom_call_target="tpu_custom_call" | custom-call | tf_op jit(solution)/shard_map/factor_apply/pallas_call | solution.py:147
Async XLA Ops:
  0.6 3.8 copy-start.2
  4.4 0.7 copy-start.3
  5.0 1.2 copy-start
  6.3 92.8 %copy-start.1 = (bf16[1,1,32,128,128]{4,3,2,1,0:T(8,128)(2,1)S(1)}, bf16[1,1,32,128,128]{4,3,2,1,0:T(8,128)(2,1)}, u32[]{:S(2)}) copy-start(bf16[1,1,32,128,128]{4,3,2,1,0:T(8,128)(2,1)} %param.5) | copy-start | bytes 3145732
  76.2 22.9 %copy-start.4 = (s32[128]{0:T(128)S(1)}, s32[128]{0:T(128)}, u32[]{:S(2)}) copy-start(s32[128]{0:T(128)} %get-tuple-element.17.refs_3_) | copy-start | bytes 1540

commit v2 on v1

--- a/solution.py
+++ b/solution.py
@@ -87,38 +87,83 @@
     )(rows_idx, cols_idx, count)
 
 
+def spread(rows, q):
+    return jnp.broadcast_to(rows[q : q + 1, :], (8, 128))
+
+
+def factor_panel(lo, a_ref, e_ref, u_ref, x_ref):
+    groups = PANEL // 8
+    first = lo < 128
+    a_half = (0, 1) if first else (1,)
+    e_half = (0,) if first else (0, 1)
+    n_a = len(a_half)
+    sub = lax.broadcasted_iota(jnp.int32, (8, 128), 0)
+
+    def rows_of(ref, g, halves):
+        return [ref[lo + 8 * g : lo + 8 * g + 8, 128 * h : 128 * h + 128] for h in halves]
+
+    rows = [rows_of(a_ref, g, a_half) + rows_of(e_ref, g, e_half) for g in range(groups)]
+    for g in range(groups):
+        c = (lo + 8 * g) % 128
+        cols = [
+            [jnp.broadcast_to(rows[i][0][:, c + q : c + q + 1], (8, 128)) for i in range(g, groups)]
+            for q in range(8)
+        ]
+        done = []
+        for q in range(8):
+            inv = lax.rsqrt(spread(cols[q][0], q))
+            cols[q] = [v * inv for v in cols[q]]
+            for p in range(q + 1, 8):
+                s = spread(cols[q][0], p)
+                cols[p] = [v - w * s for v, w in zip(cols[p], cols[q])]
+            row = [spread(v, q) for v in rows[g]]
+            for w in range(q):
+                s = spread(cols[w][0], q)
+                row = [v - s * t for v, t in zip(row, done[w])]
+            done.append([v * inv for v in row])
+        out = done[0]
+        for q in range(1, 8):
+            out = [jnp.where(sub == q, v, o) for v, o in zip(done[q], out)]
+        at = lo + 8 * g
+        for h, v in zip(a_half, out[:n_a]):
+            u_ref[at : at + 8, 128 * h : 128 * h + 128] = v
+        for h, v in zip(e_half, out[n_a:]):
+            x_ref[at : at + 8, 128 * h : 128 * h + 128] = v
+        for i in range(g + 1, groups):
+            for q in range(8):
+                rows[i] = [v - cols[q][i - g] * t for v, t in zip(rows[i], done[q])]
+    hi = lo + PANEL
+    if hi < K:
+        dn = (((0,), (0,)), ((), ()))
+        a0 = 0 if hi < 128 else 128
+        width = 128 if first else K
+        u = u_ref[lo:hi, a0:]
+        a_ref[a0:, a0:] -= lax.dot_general(u, u, dn, precision=HI, preferred_element_type=F32)
+        e_ref[a0:, :width] -= lax.dot_general(
+            u, x_ref[lo:hi, :width], dn, precision=HI, preferred_element_type=F32
+        )
+
+
+def factor_start(gram, a_ref, e_ref, u_ref, x_ref):
+    a_ref[...] = gram
+    row_i = lax.broadcasted_iota(jnp.int32, (K, K), 0)
+    col_i = lax.broadcasted_iota(jnp.int32, (K, K), 1)
+    e_ref[...] = jnp.where(row_i == col_i, 1.0, 0.0)
+    x_ref[:128, 128:] = jnp.zeros((128, 128), F32)
+    u_ref[128:, :128] = jnp.zeros((128, 128), F32)
+
+
 def factor_kernel(scale, last, *refs):
     if last:
         g_ref, y_ref, q_ref, u_ref, x_ref, a_ref, e_ref = refs
     else:
         g_ref, x_ref, u_ref, a_ref, e_ref = refs
-    n = K
-    dn = (((0,), (0,)), ((), ()))
-    a_ref[...] = g_ref[...] * scale
-    row_i = lax.broadcasted_iota(jnp.int32, (n, n), 0)
-    col_i = lax.broadcasted_iota(jnp.int32, (n, n), 1)
-    e_ref[...] = jnp.where(row_i == col_i, 1.0, 0.0)
-    sub = lax.broadcasted_iota(jnp.int32, (PANEL, 1), 0)
-    for k in range(n // PANEL):
-        lo = k * PANEL
-        r = a_ref[lo : lo + PANEL, :]
-        e = e_ref[lo : lo + PANEL, :]
-        for j in range(PANEL):
-            c = lo + j
-            inv = lax.rsqrt(r[j : j + 1, c : c + 1])
-            urow = r[j : j + 1, :] * inv
-            xrow = e[j : j + 1, :] * inv
-            f = jnp.where(sub > j, r[:, c : c + 1] * inv, 0.0)
-            r = r - f * urow
-            e = e - f * xrow
-            u_ref[c : c + 1, :] = urow
-            x_ref[c : c + 1, :] = xrow
-        if lo + PANEL < n:
-            u = u_ref[lo : lo + PANEL, :]
-            x = x_ref[lo : lo + PANEL, :]
-            a_ref[...] -= lax.dot_general(u, u, dn, precision=HI, preferred_element_type=F32)
-            e_ref[...] -= lax.dot_general(u, x, dn, precision=HI, preferred_element_type=F32)
+    factor_start(g_ref[...] * scale, a_ref, e_ref, u_ref, x_ref)
+    for lo in range(0, K, PANEL):
+        factor_panel(lo, a_ref, e_ref, u_ref, x_ref)
     if last:
+        row_i = lax.broadcasted_iota(jnp.int32, (K, K), 0)
+        col_i = lax.broadcasted_iota(jnp.int32, (K, K), 1)
         u_ref[...] = jnp.where(col_i >= row_i, u_ref[...], 0.0)
         q_ref[...] = apply_inverse(y_ref[...], x_ref[...])
 

time: 454 us -> 379 us (0.83)
  Pallas kernels: 443 us -> 368 us
    pallas_call x4, Pallas kernels: 91.6 us -> 32.2 us  [factorize(): pl.pallas_call(functools.partial(factor_kernel, scale, False), name='fact...]
    pallas_call x1, Pallas kernels: 24.3 us -> 9.44 us  [factorize(): pl.pallas_call(functools.partial(factor_kernel, scale, True), name='facto...]
where the time goes in v2:
time: 379 us; the launch traced here: 372 us
  Pallas kernels  368 us (97%)
    pallas_call x5, Pallas kernels, half_round(): pl.pallas_call(functools.partial(half_kernel, kind), name='half_' + kind,...  324 us
    pallas_call x4, Pallas kernels, factorize(): pl.pallas_call(functools.partial(factor_kernel, scale, False), name='fact...  32.2 us
    pallas_call x1, Pallas kernels, factorize(): pl.pallas_call(functools.partial(factor_kernel, scale, True), name='facto...  9.44 us

profile of v2, /device:TPU:1, one launch (start us, length us, event | category | flops | bytes accessed | tf_op | source)
XLA Modules:
  0.0 372.0 jit_solution(4749768556530585049)
XLA Ops:
  0.6 0.0 copy-start.2
  1.3 3.1 orders.1
  4.4 0.0 copy-start.3
  4.4 0.0 copy-done.2
  4.4 0.6 copy-done.3
  5.0 0.0 copy-start
  5.0 1.2 copy-done
  6.3 0.0 copy-start.1
  6.3 69.9 %half_first.1 = (f32[512,256]{1,0:T(8,128)S(1)}, f32[256,256]{1,0:T(8,128)S(1)}) custom-call(bf16[32,256]{1,0:T(8,128)(2,1)S(1)} %bitcast.11, bf16[32,128,128]{2,1,0:T(8,128)(2,1)S(1)} %bitcast.6, s32[128]{0:T(128)S(1)} %copy-done.3), custom_call_target="tpu_custom_call" | custom-call | tf_op jit(solution)/shard_map/half_first/pallas_call | solution.py:508
  76.2 0.0 copy-start.4
  76.2 8.0 %factor.4.refs_1_ = f32[256,256]{1,0:T(8,128)S(1)} custom-call(f32[256,256]{1,0:T(8,128)S(1)} %get-tuple-element.16.refs_0_), custom_call_target="tpu_custom_call" | custom-call | tf_op jit(solution)/shard_map/factor/pallas_call | solution.py:183
  84.2 0.0 copy-done.1
  84.2 0.0 copy-done.4
  84.2 62.1 %half_columns.2 = (f32[32,256]{1,0:T(8,128)S(1)}, f32[256,256]{1,0:T(8,128)S(1)}) custom-call(f32[512,256]{1,0:T(8,128)S(1)} %get-tuple-element.15.refs_0_, f32[256,256]{1,0:T(8,128)S(1)} %factor.4.refs_1_, bf16[32,128,128]{2,1,0:T(8,128)(2,1)S(1)} %bitcast.7, s32[128]{0:T(128)S(1)} %copy-done.4), custom_call_target="tpu_custom_call" | custom-call | tf_op jit(solution)/shard_map/half_columns/pallas_call | solution.py:508
  146.4 8.0 %factor.5.refs_1_ = f32[256,256]{1,0:T(8,128)S(1)} custom-call(f32[256,256]{1,0:T(8,128)S(1)} %get-tuple-element.19.refs_0_), custom_call_target="tpu_custom_call" | custom-call | tf_op jit(solution)/shard_map/factor/pallas_call | solution.py:183
  154.5 65.1 %half_rows.2 = (f32[512,256]{1,0:T(8,128)S(1)}, f32[256,256]{1,0:T(8,128)S(1)}) custom-call(f32[32,256]{1,0:T(8,128)S(1)} %get-tuple-element.18.refs_0_, f32[256,256]{1,0:T(8,128)S(1)} %factor.5.refs_1_, bf16[32,128,128]{2,1,0:T(8,128)(2,1)S(1)} %bitcast.8, s32[128]{0:T(128)S(1)} %copy-done.3), custom_call_target="tpu_custom_call" | custom-call | tf_op jit(solution)/shard_map/half_rows/pallas_call | solution.py:508
  219.5 8.0 %factor.6.refs_1_ = f32[256,256]{1,0:T(8,128)S(1)} custom-call(f32[256,256]{1,0:T(8,128)S(1)} %get-tuple-element.21.refs_0_), custom_call_target="tpu_custom_call" | custom-call | tf_op jit(solution)/shard_map/factor/pallas_call | solution.py:183
  227.6 62.1 %half_columns.3 = (f32[32,256]{1,0:T(8,128)S(1)}, f32[256,256]{1,0:T(8,128)S(1)}) custom-call(f32[512,256]{1,0:T(8,128)S(1)} %get-tuple-element.20.refs_0_, f32[256,256]{1,0:T(8,128)S(1)} %factor.6.refs_1_, bf16[32,128,128]{2,1,0:T(8,128)(2,1)S(1)} %bitcast.9, s32[128]{0:T(128)S(1)} %copy-done.4), custom_call_target="tpu_custom_call" | custom-call | tf_op jit(solution)/shard_map/half_columns/pallas_call | solution.py:508
  289.7 8.0 %factor.7.refs_1_ = f32[256,256]{1,0:T(8,128)S(1)} custom-call(f32[256,256]{1,0:T(8,128)S(1)} %get-tuple-element.23.refs_0_), custom_call_target="tpu_custom_call" | custom-call | tf_op jit(solution)/shard_map/factor/pallas_call | solution.py:183
  297.8 64.5 %half_rows.3 = (f32[512,256]{1,0:T(8,128)S(1)}, f32[256,256]{1,0:T(8,128)S(1)}) custom-call(f32[32,256]{1,0:T(8,128)S(1)} %get-tuple-element.22.refs_0_, f32[256,256]{1,0:T(8,128)S(1)} %factor.7.refs_1_, bf16[32,128,128]{2,1,0:T(8,128)(2,1)S(1)} %bitcast.10, s32[128]{0:T(128)S(1)} %copy-done.3), custom_call_target="tpu_custom_call" | custom-call | tf_op jit(solution)/shard_map/half_rows/pallas_call | solution.py:508
  362.3 9.4 %factor_apply.1 = (f32[512,256]{1,0:T(8,128)}, f32[256,256]{1,0:T(8,128)}) custom-call(f32[256,256]{1,0:T(8,128)S(1)} %get-tuple-element.24.refs_0_, f32[512,256]{1,0:T(8,128)S(1)} %get-tuple-element.25.refs_1_), custom_call_target="tpu_custom_call" | custom-call | tf_op jit(solution)/shard_map/factor_apply/pallas_call | solution.py:192
Async XLA Ops:
  0.6 3.8 %copy-start.2 = (bf16[1,32,256]{2,1,0:T(8,128)(2,1)S(1)}, bf16[1,32,256]{2,1,0:T(8,128)(2,1)}, u32[]{:S(2)}) copy-start(bf16[1,32,256]{2,1,0:T(8,128)(2,1)} %param.9) | copy-start | bytes 49156
  4.4 0.7 copy-start.3
  5.0 1.2 copy-start
  6.3 78.0 %copy-start.1 = (bf16[1,1,32,128,128]{4,3,2,1,0:T(8,128)(2,1)S(1)}, bf16[1,1,32,128,128]{4,3,2,1,0:T(8,128)(2,1)}, u32[]{:S(2)}) copy-start(bf16[1,1,32,128,128]{4,3,2,1,0:T(8,128)(2,1)} %param.5) | copy-start | bytes 3145732
  76.2 8.1 %copy-start.4 = (s32[128]{0:T(128)S(1)}, s32[128]{0:T(128)}, u32[]{:S(2)}) copy-start(s32[128]{0:T(128)} %get-tuple-element.17.refs_3_) | copy-start | bytes 1540
